TPU v7x, 256 devices: a whole 4x4x8 slice. The times are simulated.
256 devices in a mesh: space: 16 (over z, y_hi), leaf: 16 (over x, y_lo, core).
Axes of the slice: x: 4, y: 4 (y_hi: 2, y_lo: 2; y = y_hi * 2 + y_lo), z: 8, core: 2. Of those that a mesh axis runs over, the one named last changes fastest.
Arguments:
- charges: bfloat16 [16, 2097152], P(None, ('space', 'leaf')), may hold values from -6 to 6
- leaf_basis: bfloat16 [16384, 64, 128], P(('space', 'leaf')), may hold values from -0.5 to 0.5
- transfer_one: bfloat16 [2048, 64, 512], P(('space', 'leaf')), may hold values from -0.25 to 0.25
- transfer_two: bfloat16 [256, 64, 512], P(('space', 'leaf')), may hold values from -0.25 to 0.25
- nodes_leaf: bfloat16 [16384, 3, 64], P(('space', 'leaf')), may hold values from 0 to 6
- nodes_one: bfloat16 [2048, 3, 64], P(('space', 'leaf')), may hold values from 0 to 6
- nodes_two: bfloat16 [256, 3, 64], P(('space', 'leaf')), may hold values from 0 to 6
- links_leaf: int32 [16384, 96], P(('space', 'leaf')), may hold values from -1 to 16383, as said below
- links_one: int32 [2048, 96], P(('space', 'leaf')), may hold values from -1 to 2047, as said below
- links_two: int32 [256, 96], P(('space', 'leaf')), may hold values from -1 to 255, as said below
Outputs:
- potentials: bfloat16 [16, 2097152], P(None, ('space', 'leaf'))
Inputs may be any that keep to these rules, and one draw needn't show every extreme that they name: `links_leaf`: A live source leaf lies on a device whose space index differs from that of the target leaf's device by at most one; live slots of a row come first. `links_one`: A live source cluster lies on a device whose space index differs from that of the target's device by at most one; live slots of a row come first. `links_two`: live slots of a row come first.
All inputs are finite; a program needn't handle non-finite values.
Results may differ from a plain program's by a relative error of at most 0.007.
Values may be sent and summed in bfloat16 or wider, within the bound.
A program may use at most 128 MiB of HBM per device.

v0:
```python
import jax
import jax.numpy as jnp
from jax import lax
from jax.sharding import PartitionSpec as P

SQRT_THREE = 1.7320508075688772
LENGTH = 2.0
AMPLITUDE = 0.25


def with_halo(cells, sides, width):
    for axis, dim in sides:
        count = lax.axis_size(axis)
        ends = count - 1
        head = lax.slice_in_dim(cells, 0, width, axis=dim)
        tail = lax.slice_in_dim(cells, cells.shape[dim] - width, cells.shape[dim], axis=dim)
        cells = jnp.concatenate(
            [
                lax.ppermute(tail, axis, [(i, (i + 1) % count) for i in range(ends)]),
                cells,
                lax.ppermute(head, axis, [((i + 1) % count, i) for i in range(ends)]),
            ],
            axis=dim,
        )
    return cells


def matern_block(target_nodes, source_nodes):
    diff = target_nodes[:, None, :, :, None] - source_nodes[:, :, :, None, :]
    dist = jnp.sqrt(jnp.sum(diff * diff, axis=2)) * (SQRT_THREE / LENGTH)
    return (AMPLITUDE * (1.0 + dist) * jnp.exp(-dist)).astype(jnp.bfloat16)


def couple(table_coef, table_nodes, rows, live, target_nodes, rank, width):
    count = rows.shape[0]
    slots = rows.shape[1]
    group = min(count, 4)

    def one_group(args):
        index, alive, tnodes = args
        picked = table_coef[index].reshape(group, slots, rank, width)
        picked = jnp.where(alive[:, :, None, None], picked, jnp.zeros((), jnp.bfloat16))
        source_nodes = table_nodes[index].astype(jnp.float32)
        matrix = matern_block(tnodes.astype(jnp.float32), source_nodes)
        return jnp.einsum("gjab,gjbv->gav", matrix, picked, preferred_element_type=jnp.float32)

    result = lax.map(
        one_group,
        (
            rows.reshape(-1, group, slots),
            live.reshape(-1, group, slots),
            target_nodes.reshape(-1, group, 3, rank),
        ),
    )
    return result.reshape(count, rank, width)


def local(
    charges,
    leaf_basis,
    transfer_one,
    transfer_two,
    nodes_leaf,
    nodes_one,
    nodes_two,
    links_leaf,
    links_one,
    links_two,
):
    width = charges.shape[0]
    leaf_dev = leaf_basis.shape[0]
    rank = leaf_basis.shape[1]
    leaf_size = leaf_basis.shape[2]
    one_dev = leaf_dev // 8
    two_dev = one_dev // 8
    n_leaf = lax.axis_size("leaf")
    my_space = lax.axis_index("space")
    shaped = charges.reshape(width, leaf_dev, leaf_size)
    coef_leaf = jnp.einsum(
        "tkp,vtp->tkv", leaf_basis, shaped, preferred_element_type=jnp.float32
    ).astype(jnp.bfloat16)
    coef_one = jnp.einsum(
        "pkm,pmv->pkv",
        transfer_one,
        coef_leaf.reshape(one_dev, 8 * rank, width),
        preferred_element_type=jnp.float32,
    ).astype(jnp.bfloat16)
    coef_two = jnp.einsum(
        "pkm,pmv->pkv",
        transfer_two,
        coef_one.reshape(two_dev, 8 * rank, width),
        preferred_element_type=jnp.float32,
    ).astype(jnp.bfloat16)
    flat_leaf = coef_leaf.reshape(leaf_dev, rank * width)
    whole_coef, whole_nodes = (
        lax.all_gather(flat_leaf, "leaf", axis=0, tiled=True),
        lax.all_gather(nodes_leaf, "leaf", axis=0, tiled=True),
    )
    near_coef, near_nodes = (
        with_halo(whole_coef[None], (("space", 0),), 1),
        with_halo(whole_nodes[None], (("space", 0),), 1),
    )
    live_leaf = links_leaf >= 0
    safe_leaf = jnp.where(live_leaf, links_leaf, 0)
    owner = safe_leaf // leaf_dev
    rows_leaf = (
        (owner // n_leaf - my_space + 1) * (n_leaf * leaf_dev)
        + owner % n_leaf * leaf_dev
        + safe_leaf % leaf_dev
    )
    rows_leaf = jnp.where(live_leaf, rows_leaf, 0)
    far_leaf = couple(
        near_coef.reshape(-1, rank * width),
        near_nodes.reshape(-1, 3, rank),
        rows_leaf,
        live_leaf,
        nodes_leaf,
        rank,
        width,
    )
    flat_one = coef_one.reshape(one_dev, rank * width)
    block_coef, block_nodes = (
        lax.all_gather(flat_one, "leaf", axis=0, tiled=True),
        lax.all_gather(nodes_one, "leaf", axis=0, tiled=True),
    )
    band_coef, band_nodes = (
        with_halo(block_coef[None], (("space", 0),), 1),
        with_halo(block_nodes[None], (("space", 0),), 1),
    )
    live_one = links_one >= 0
    safe_one = jnp.where(live_one, links_one, 0)
    owner_one = safe_one // one_dev
    rows_one = (
        (owner_one // n_leaf - my_space + 1) * (n_leaf * one_dev)
        + owner_one % n_leaf * one_dev
        + safe_one % one_dev
    )
    rows_one = jnp.where(live_one, rows_one, 0)
    far_one = couple(
        band_coef.reshape(-1, rank * width),
        band_nodes.reshape(-1, 3, rank),
        rows_one,
        live_one,
        nodes_one,
        rank,
        width,
    )
    flat_two = coef_two.reshape(two_dev, rank * width)
    every_coef, every_nodes = (
        lax.all_gather(flat_two, ("space", "leaf"), axis=0, tiled=True),
        lax.all_gather(nodes_two, ("space", "leaf"), axis=0, tiled=True),
    )
    live_two = links_two >= 0
    rows_two = jnp.where(live_two, links_two, 0)
    far_two = couple(every_coef, every_nodes, rows_two, live_two, nodes_two, rank, width)
    local_two = far_two.astype(jnp.bfloat16)
    down_one = jnp.einsum(
        "pkm,pkv->pmv", transfer_two, local_two, preferred_element_type=jnp.float32
    )
    local_one = (far_one + down_one.reshape(one_dev, rank, width)).astype(jnp.bfloat16)
    down_leaf = jnp.einsum(
        "pkm,pkv->pmv", transfer_one, local_one, preferred_element_type=jnp.float32
    )
    local_leaf = (far_leaf + down_leaf.reshape(leaf_dev, rank, width)).astype(jnp.bfloat16)
    result = jnp.einsum("tkp,tkv->vtp", leaf_basis, local_leaf, preferred_element_type=jnp.float32)
    return result.reshape(width, leaf_dev * leaf_size).astype(jnp.bfloat16)


def solution(mesh):
    return jax.shard_map(
        local,
        mesh=mesh,
        in_specs=(
            P(None, ("space", "leaf")),
            P(("space", "leaf"), None, None),
            P(("space", "leaf"), None, None),
            P(("space", "leaf"), None, None),
            P(("space", "leaf"), None, None),
            P(("space", "leaf"), None, None),
            P(("space", "leaf"), None, None),
            P(("space", "leaf"), None),
            P(("space", "leaf"), None),
            P(("space", "leaf"), None),
        ),
        out_specs=P(None, ("space", "leaf")),
        check_vma=False,
    )
```

profile of v0, /device:TPU:137, one launch (start us, length us, event | category | flops | bytes accessed | tf_op | source)
XLA Modules:
  0.0 1369.0 jit_solution(4095242045511093542)
XLA Ops:
  10.6 17.4 %all_gather.20 = bf16[128,3,64]{2,0,1:T(8,128)(2,1)S(1)} all-gather(bf16[8,3,64]{2,0,1:T(8,128)(2,1)} %param.19), channel_id=1, replica_groups=mesh['space'=16,'leaf'=16] {'leaf'}, dimensions={0}, use_global_device_ids=true | all-gather | bytes 52224 | tf_op jit(solution)/shard_map/all_gather | solution.py:124
  36.7 21.0 %all_gather.21 = bf16[128,1024]{1,0:T(8,128)(2,1)S(1)} all-gather(bf16[8,1024]{1,0:T(8,128)(2,1)S(1)} %reshape.238), channel_id=1, replica_groups=mesh['space'=16,'leaf'=16] {'leaf'}, dimensions={0}, use_global_device_ids=true | all-gather | bytes 278528 | tf_op jit(solution)/shard_map/all_gather | solution.py:123
  66.1 26.5 %all_gather.18 = bf16[1024,3,64]{2,1,0:T(4,128)(2,1)S(1)} all-gather(bf16[64,3,64]{2,1,0:T(4,128)(2,1)S(1)} %copy.244), channel_id=1, replica_groups=mesh['space'=16,'leaf'=16] {'leaf'}, dimensions={0}, use_global_device_ids=true | all-gather | bytes 417792 | tf_op jit(solution)/shard_map/all_gather | solution.py:97
  95.8 340.5 %all_gather.22 = bf16[256,3,64]{2,1,0:T(4,128)(2,1)S(1)} all-gather(bf16[1,3,64]{2,1,0:T(4,128)(2,1)S(1)} %copy-done.10), channel_id=1, replica_groups=mesh['space'=16,'leaf'=16] {'space','leaf'}, dimensions={0}, use_global_device_ids=true | all-gather | bytes 98688 | tf_op jit(solution)/shard_map/all_gather | solution.py:151
  437.6 349.1 %all-gather = bf16[256,1,1024]{2,1,0:T(2,128)(2,1)S(1)} all-gather(bf16[1,1,1024]{2,1,0:T(2,128)(2,1)S(1)} %reshape.311), channel_id=1, replica_groups=mesh['space'=16,'leaf'=16] {'space','leaf'}, dimensions={0}, use_global_device_ids=true | all-gather | bytes 526336 | tf_op jit(solution)/shard_map/all_gather | solution.py:150
  797.6 7.0 collective-permute-start.3
  806.5 70.0 %while.25 = (s32[]{:T(128)}, f32[2,4,64,16]{2,3,1,0:T(8,128)}, bf16[2,4,3,64]{3,2,1,0:T(4,128)(2,1)S(1)}, s32[2,4,96]{2,1,0:T(4,128)S(1)}, bf16[384,3,64]{2,1,0:...) while((s32[]{:T(128)}, f32[2,4,64,16]{2,3,1,0:T(8,128)}, ...), condition=%wide.region_5.6_spmd, body=%wide.region_3.5_spmd.sunk | while | flops 72747904 | bytes 27565348 | solution.py:47
  819.4 6.5 multiply_reduce_fusion.6
  825.9 7.7 multiply_convert_fusion.6
  849.1 6.5 multiply_reduce_fusion.6
  855.6 7.7 multiply_convert_fusion.6
  887.6 12.3 collective-permute-done.3
  905.5 453.9 %while.24 = (s32[]{:T(128)}, f32[16,4,64,16]{2,1,0,3:T(4,128)}, bf16[16,4,3,64]{3,2,1,0:T(4,128)(2,1)S(1)}, s32[16,4,96]{2,1,0:T(4,128)}, bf16[3072,3,64]{2,1,0:...) while((s32[]{:T(128)}, f32[16,4,64,16]{2,1,0,3:T(4,128)}, ...), condition=%wide.region_2.3_spmd, body=%wide.region_0.2_spmd.sunk | while | flops 72747904 | bytes 27270436 | solution.py:47
  919.0 6.4 gather_fusion.1
  947.4 6.4 gather_fusion.1
  975.8 6.4 gather_fusion.1
  1004.2 6.4 gather_fusion.1
  1032.6 6.4 gather_fusion.1
  1061.0 6.4 gather_fusion.1
  1089.3 6.4 gather_fusion.1
  1117.6 6.4 gather_fusion.1
  1146.0 6.4 gather_fusion.1
  1174.4 6.4 gather_fusion.1
  1287.8 6.4 gather_fusion.1
  (407 shorter events, 471.0 us)
Async XLA Ops:
  6.5 89.3 %copy-start.10 = (bf16[1,3,64]{2,1,0:T(4,128)(2,1)S(1)}, bf16[1,3,64]{2,1,0:T(4,128)(2,1)}, u32[]{:S(2)}) copy-start(bf16[1,3,64]{2,1,0:T(4,128)(2,1)} %param.20) | copy-start | bytes 1156
  6.5 429.8 %copy-start.11 = (s32[1,96]{1,0:T(1,128)S(1)}, s32[1,96]{1,0:T(1,128)}, u32[]{:S(2)}) copy-start(s32[1,96]{1,0:T(1,128)} %param.23) | copy-start | bytes 1156
  6.5 430.7 %copy-start.5 = (bf16[1,64,512]{2,1,0:T(8,128)(2,1)S(1)}, bf16[1,64,512]{2,1,0:T(8,128)(2,1)}, u32[]{:S(2)}) copy-start(bf16[1,64,512]{2,1,0:T(8,128)(2,1)} %param.17) | copy-start | bytes 196612
  6.5 791.0 %all-gather.3.cloned.1.call-start = ((), (), s32[]{:S(2)}) async-start(), calls=%async_computation | async-start | bytes 2228224 | tf_op jit(solution)/shard_map/all_gather | solution.py:96
  9.3 778.5 %copy-start.9 = (s32[8,96]{1,0:T(8,128)S(1)}, s32[8,96]{1,0:T(8,128)}, u32[]{:S(2)}) copy-start(s32[8,96]{1,0:T(8,128)} %param.22) | copy-start | bytes 9220
  9.3 779.1 %copy-start.6 = (s32[64,96]{1,0:T(8,128)S(1)}, s32[64,96]{1,0:T(8,128)}, u32[]{:S(2)}) copy-start(s32[64,96]{1,0:T(8,128)} %param.21) | copy-start | bytes 73732
  28.0 765.2 %collective-permute-start.5 = (bf16[1,128,3,64]{3,1,2,0:T(8,128)(2,1)S(1)}, bf16[1,128,3,64]{3,1,2,0:T(8,128)(2,1)}, u32[]{:S(2)}, u32[]{:S(2)}) collective-permute-start(bf16[1,128,3,64]{3,1,2,0:T(8,128)(2,1)S(1)} %bitcast.156), channel_id=1, source_target_pairs={{16,0},{32,16},{48,32},{64,48},{80,64},{96,80},{112,96},{128,112},... | collective-permute-start | bytes 147464 | tf_op jit(solution)/shard_map/ppermute | solution.py:21
  31.8 763.3 %collective-permute-start.4 = (bf16[1,128,3,64]{3,1,2,0:T(8,128)(2,1)S(1)}, bf16[1,128,3,64]{3,1,2,0:T(8,128)(2,1)}, u32[]{:S(2)}, u32[]{:S(2)}) collective-permute-start(bf16[1,128,3,64]{3,1,2,0:T(8,128)(2,1)S(1)} %bitcast.157), channel_id=1, source_target_pairs={{0,16},{16,32},{32,48},{48,64},{64,80},{80,96},{96,112},{112,128},... | collective-permute-start | bytes 147464 | tf_op jit(solution)/shard_map/ppermute | solution.py:19
  57.7 738.7 %collective-permute-start.7 = (bf16[1,128,1024]{2,1,0:T(8,128)(2,1)S(1)}, bf16[1,128,1024]{2,1,0:T(8,128)(2,1)}, u32[]{:S(2)}, u32[]{:S(2)}) collective-permute-start(bf16[1,128,1024]{2,1,0:T(8,128)(2,1)S(1)} %bitcast.151), channel_id=1, source_target_pairs={{16,0},{32,16},{48,32},{64,48},{80,64},{96,80},{112,96},{128,112},... | collective-permute-start | bytes 786440 | tf_op jit(solution)/shard_map/ppermute | solution.py:21
  63.3 733.1 %collective-permute-start.6 = (bf16[1,128,1024]{2,1,0:T(8,128)(2,1)S(1)}, bf16[1,128,1024]{2,1,0:T(8,128)(2,1)}, u32[]{:S(2)}, u32[]{:S(2)}) collective-permute-start(bf16[1,128,1024]{2,1,0:T(8,128)(2,1)S(1)} %bitcast.152), channel_id=1, source_target_pairs={{0,16},{16,32},{32,48},{48,64},{64,80},{80,96},{96,112},{112,128},... | collective-permute-start | bytes 786440 | tf_op jit(solution)/shard_map/ppermute | solution.py:19
  92.6 699.0 %copy-start.1 = (bf16[1024,3,64]{2,1,0:T(4,128)(2,1)}, bf16[1024,3,64]{2,1,0:T(4,128)(2,1)S(1)}, u32[]{:S(2)}) copy-start(bf16[1024,3,64]{2,1,0:T(4,128)(2,1)S(1)} %all_gather.18) | copy-start | bytes 1179652
  93.8 785.2 %collective-permute-start.1 = (bf16[1,1024,3,64]{1,3,2,0:T(8,128)(2,1)}, bf16[1,1024,3,64]{1,3,2,0:T(8,128)(2,1)}, u32[]{:S(2)}, u32[]{:S(2)}) collective-permute-start(bf16[1,1024,3,64]{1,3,2,0:T(8,128)(2,1)} %copy.246), channel_id=1, source_target_pairs={{16,0},{32,16},{48,32},{64,48},{80,64},{96,80},{112,96},{128,112},... | collective-permute-start | bytes 1179656 | tf_op jit(solution)/shard_map/ppermute | solution.py:21
  793.2 87.4 %collective-permute-start = (bf16[1,1024,3,64]{1,3,2,0:T(8,128)(2,1)}, bf16[1,1024,3,64]{1,3,2,0:T(8,128)(2,1)}, u32[]{:S(2)}, u32[]{:S(2)}) collective-permute-start(bf16[1,1024,3,64]{1,3,2,0:T(8,128)(2,1)} %copy.246), channel_id=1, source_target_pairs={{0,16},{16,32},{32,48},{48,64},{64,80},{80,96},{96,112},{112,128},... | collective-permute-start | bytes 1179656 | tf_op jit(solution)/shard_map/ppermute | solution.py:19
  797.6 102.4 %collective-permute-start.3 = (bf16[1,1024,1024]{2,1,0:T(8,128)(2,1)}, bf16[1,1024,1024]{2,1,0:T(8,128)(2,1)}, u32[]{:S(2)}, u32[]{:S(2)}) collective-permute-start(bf16[1,1024,1024]{2,1,0:T(8,128)(2,1)} %bitcast.147), channel_id=1, source_target_pairs={{16,0},{32,16},{48,32},{64,48},{80,64},{96,80},{112,96},{128,112},... | collective-permute-start | bytes 6291464 | tf_op jit(solution)/shard_map/ppermute | solution.py:21
  804.5 95.4 %collective-permute-start.2 = (bf16[1,1024,1024]{2,1,0:T(8,128)(2,1)}, bf16[1,1024,1024]{2,1,0:T(8,128)(2,1)}, u32[]{:S(2)}, u32[]{:S(2)}) collective-permute-start(bf16[1,1024,1024]{2,1,0:T(8,128)(2,1)} %bitcast.148), channel_id=1, source_target_pairs={{0,16},{16,32},{32,48},{48,64},{64,80},{80,96},{96,112},{112,128},... | collective-permute-start | bytes 6291464 | tf_op jit(solution)/shard_map/ppermute | solution.py:19
  882.2 17.7 %copy-start.2 = (bf16[1024,1024]{1,0:T(8,128)(2,1)S(1)}, bf16[1024,1024]{1,0:T(8,128)(2,1)}, u32[]{:S(2)}) copy-start(bf16[1024,1024]{1,0:T(8,128)(2,1)} %all-gather.3.cloned.1.call-done) | copy-start | bytes 6291460
  953.8 8.5 copy-start.4
  982.2 8.5 copy-start.4
  1010.6 8.4 copy-start.4
  1038.9 8.5 copy-start.4
  1124.0 8.5 copy-start.4
  1152.4 8.5 copy-start.4
  1294.1 8.5 copy-start.4
  1322.6 8.5 copy-start.4
  (29 other events, 145.9 us)
Sparse Core Ops, SparseCore 0:
  10.7 40.2 all-gather.2
where the time goes:
time: 1380 us; the launch traced here: 1370 us
  blocking collectives  755 us (55%)
  local copies, waits for them, and re-layouts  224 us (16%)
  other arithmetic  216 us (16%)
  matrix products  109 us (8%)
  starting transfers between devices  27 us (2%)
  between operations  14.1 us (1%)
    all_gather x1, blocking collectives, local(): lax.all_gather(flat_two, ('space', 'leaf'), axis=0, tiled=True)  349 us
    all_gather x1, blocking collectives, local(): lax.all_gather(nodes_two, ('space', 'leaf'), axis=0, tiled=True)  341 us
    gather x38, local copies, waits for them, and re-layouts, one_group(): picked = table_coef[index].reshape(group, slots, rank, width)  115 us
    dot_general x19, matrix products, one_group(): jnp.einsum('gjab,gjbv->gav', matrix, picked, preferred_element_type=jnp.f...  104 us
    convert_element_type x19, other arithmetic, matern_block(): return (AMPLITUDE * (1.0 + dist) * jnp.exp(-dist)).astype(jnp.bfloat16)  103 us
    reduce_sum x19, other arithmetic, matern_block(): dist = jnp.sqrt(jnp.sum(diff * diff, axis=2)) * (SQRT_THREE / LENGTH)  66.6 us
    gather x20, local copies, waits for them, and re-layouts, one_group(): source_nodes = table_nodes[index].astype(jnp.float32)  54.8 us
  transfers between devices with their start and end apart: 9, of which 1 were waited for; matrix products, arithmetic and copies ran while one was open for 6% of the time, Pallas kernels for 0%

commit v1 on v0

--- a/solution.py
+++ b/solution.py
@@ -147,7 +147,12 @@
     )
     flat_two = coef_two.reshape(two_dev, rank * width)
     every_coef, every_nodes = (
-        lax.all_gather(flat_two, ("space", "leaf"), axis=0, tiled=True),
+        jnp.concatenate(
+            lax.all_to_all(
+                jnp.stack([flat_two] * lax.axis_size(("space", "leaf"))), ("space", "leaf"), 0, 0
+            ),
+            axis=0,
+        ),
         lax.all_gather(nodes_two, ("space", "leaf"), axis=0, tiled=True),
     )
     live_two = links_two >= 0

time: 1380 us -> 1070 us (0.78)
  blocking collectives: 755 us -> 417 us
  starting transfers between devices: 27 us -> 41.7 us
    all_gather x1 -> x0, blocking collectives: 349 us -> none  [local(): lax.all_gather(flat_two, ('space', 'leaf'), axis=0, tiled=True)]
    all_to_all x0 -> x1, starting transfers between devices: none -> 14.6 us  [local(): lax.all_to_all(jnp.stack([flat_two] * lax.axis_size(('space', 'leaf'))),...]
  transfers between devices with their start and end apart: 9 -> 10, of which waited for: 1 -> 1; matrix products, arithmetic and copies ran while one was open for 6% -> 9% of each run, Pallas kernels for 0% -> 0%
where the time goes in v1:
time: 1070 us; the launch traced here: 1060 us
  blocking collectives  417 us (39%)
  local copies, waits for them, and re-layouts  231 us (22%)
  other arithmetic  225 us (21%)
  matrix products  109 us (10%)
  starting transfers between devices  41.7 us (4%)
  waiting for transfers between devices  18.8 us (2%)
  between operations  13.9 us (1%)
    all_gather x1, blocking collectives, local(): lax.all_gather(nodes_two, ('space', 'leaf'), axis=0, tiled=True)  352 us
    gather x38, local copies, waits for them, and re-layouts, one_group(): picked = table_coef[index].reshape(group, slots, rank, width)  115 us
    dot_general x19, matrix products, one_group(): jnp.einsum('gjab,gjbv->gav', matrix, picked, preferred_element_type=jnp.f...  105 us
    convert_element_type x19, other arithmetic, matern_block(): return (AMPLITUDE * (1.0 + dist) * jnp.exp(-dist)).astype(jnp.bfloat16)  104 us
    reduce_sum x19, other arithmetic, matern_block(): dist = jnp.sqrt(jnp.sum(diff * diff, axis=2)) * (SQRT_THREE / LENGTH)  66.6 us
    gather x20, local copies, waits for them, and re-layouts, one_group(): source_nodes = table_nodes[index].astype(jnp.float32)  54.8 us
    all_gather x1, blocking collectives, local(): lax.all_gather(nodes_leaf, 'leaf', axis=0, tiled=True)  25.9 us
  transfers between devices with their start and end apart: 10, of which 1 were waited for; matrix products, arithmetic and copies ran while one was open for 9% of the time, Pallas kernels for 0%

profile of v1, /device:TPU:137, one launch (start us, length us, event | category | flops | bytes accessed | tf_op | source)
XLA Modules:
  0.0 1056.7 jit_solution(5471091866150547112)
XLA Ops:
  10.6 17.4 %all_gather.17 = bf16[128,3,64]{2,0,1:T(8,128)(2,1)S(1)} all-gather(bf16[8,3,64]{2,0,1:T(8,128)(2,1)} %param.19), channel_id=1, replica_groups=mesh['space'=16,'leaf'=16] {'leaf'}, dimensions={0}, use_global_device_ids=true | all-gather | bytes 52224 | tf_op jit(solution)/shard_map/all_gather | solution.py:124
  36.7 21.0 %all_gather.18 = bf16[128,1024]{1,0:T(8,128)(2,1)S(1)} all-gather(bf16[8,1024]{1,0:T(8,128)(2,1)S(1)} %reshape.242), channel_id=1, replica_groups=mesh['space'=16,'leaf'=16] {'leaf'}, dimensions={0}, use_global_device_ids=true | all-gather | bytes 278528 | tf_op jit(solution)/shard_map/all_gather | solution.py:123
  66.7 25.9 %all_gather.15 = bf16[1024,3,64]{2,1,0:T(4,128)(2,1)S(1)} all-gather(bf16[64,3,64]{2,1,0:T(4,128)(2,1)} %copy.242), channel_id=1, replica_groups=mesh['space'=16,'leaf'=16] {'leaf'}, dimensions={0}, use_global_device_ids=true | all-gather | bytes 417792 | tf_op jit(solution)/shard_map/all_gather | solution.py:97
  104.1 14.6 %all-to-all-start = ((bf16[256,2,512]{2,1,0:T(2,128)(2,1)}), bf16[256,2,512]{2,1,0:T(2,128)(2,1)}, u32[]{:S(2)}, u32[]{:S(2)}) async-start(bf16[256,2,512]{2,1,0:T(2,128)(2,1)} %reshape.319), calls=%async_computation | async-start | bytes 1048576 | tf_op jit(solution)/shard_map/all_to_all | solution.py:151
  118.7 352.3 %all_gather.19 = bf16[256,3,64]{2,1,0:T(4,128)(2,1)S(1)} all-gather(bf16[1,3,64]{2,1,0:T(4,128)(2,1)S(1)} %copy-done.10), channel_id=1, replica_groups=mesh['space'=16,'leaf'=16] {'space','leaf'}, dimensions={0}, use_global_device_ids=true | all-gather | bytes 98688 | tf_op jit(solution)/shard_map/all_gather | solution.py:156
  485.2 7.0 collective-permute-start.3
  494.2 58.0 %while.25 = (s32[]{:T(128)}, f32[2,4,64,16]{2,3,1,0:T(8,128)}, bf16[2,4,3,64]{3,2,1,0:T(4,128)(2,1)S(1)}, s32[2,4,96]{2,1,0:T(4,128)S(1)}, bf16[384,3,64]{2,1,0:...) while((s32[]{:T(128)}, f32[2,4,64,16]{2,3,1,0:T(8,128)}, ...), condition=%wide.region_5.6_spmd, body=%wide.region_3.5_spmd.sunk | while | flops 72747904 | bytes 27568448 | solution.py:47
  496.5 6.5 multiply_reduce_fusion.6
  503.0 7.6 multiply_convert_fusion.6
  525.5 6.5 multiply_reduce_fusion.6
  532.0 7.6 multiply_convert_fusion.6
  568.9 18.8 %collective-permute-done.3 = bf16[1,1024,1024]{2,1,0:T(8,128)(2,1)} collective-permute-done((bf16[1,1024,1024]{2,1,0:T(8,128)(2,1)}, bf16[1,1024,1024]{2,1,0:T(8,128)(2,1)}, u32[]{:S(2)}, u32[]{:S(2)}) %collective-permute-start.3) | collective-permute-done | bytes 2097184 | tf_op jit(solution)/shard_map/ppermute | solution.py:21
  587.6 6.4 pad_maximum_fusion
  594.1 453.2 %while.24 = (s32[]{:T(128)}, f32[16,4,64,16]{2,1,0,3:T(4,128)}, bf16[16,4,3,64]{3,2,1,0:T(4,128)(2,1)}, s32[16,4,96]{2,1,0:T(4,128)}, bf16[3072,3,64]{2,1,0:T(4,...) while((s32[]{:T(128)}, f32[16,4,64,16]{2,1,0,3:T(4,128)}, ...), condition=%wide.region_2.3_spmd, body=%wide.region_0.2_spmd.sunk | while | flops 72747904 | bytes 27073772 | solution.py:47
  607.6 6.4 gather_fusion.1
  636.0 6.4 gather_fusion.1
  664.3 6.4 gather_fusion.1
  692.7 6.4 gather_fusion.1
  720.9 6.4 gather_fusion.1
  749.2 6.4 gather_fusion.1
  777.6 6.4 gather_fusion.1
  805.8 6.4 gather_fusion.1
  834.2 6.4 gather_fusion.1
  862.5 6.4 gather_fusion.1
  (359 shorter events, 486.7 us)
Async XLA Ops:
  6.5 89.4 %copy-start.4 = (bf16[1,64,512]{2,1,0:T(8,128)(2,1)S(1)}, bf16[1,64,512]{2,1,0:T(8,128)(2,1)}, u32[]{:S(2)}) copy-start(bf16[1,64,512]{2,1,0:T(8,128)(2,1)} %param.17) | copy-start | bytes 196612
  6.5 112.2 %copy-start.10 = (bf16[1,3,64]{2,1,0:T(4,128)(2,1)S(1)}, bf16[1,3,64]{2,1,0:T(4,128)(2,1)}, u32[]{:S(2)}) copy-start(bf16[1,3,64]{2,1,0:T(4,128)(2,1)} %param.20) | copy-start | bytes 1156
  6.5 464.5 %copy-start.12 = (s32[1,96]{1,0:T(1,128)S(1)}, s32[1,96]{1,0:T(1,128)}, u32[]{:S(2)}) copy-start(s32[1,96]{1,0:T(1,128)} %param.23) | copy-start | bytes 1156
  6.5 465.4 %copy-start.9 = (s32[8,96]{1,0:T(8,128)S(1)}, s32[8,96]{1,0:T(8,128)}, u32[]{:S(2)}) copy-start(s32[8,96]{1,0:T(8,128)} %param.22) | copy-start | bytes 9220
  6.5 478.7 %all-gather.2.cloned.1.call-start = ((), (), s32[]{:S(2)}) async-start(), calls=%async_computation.1 | async-start | bytes 2228224 | tf_op jit(solution)/shard_map/all_gather | solution.py:96
  28.0 452.9 %collective-permute-start.5 = (bf16[1,128,3,64]{3,1,2,0:T(8,128)(2,1)S(1)}, bf16[1,128,3,64]{3,1,2,0:T(8,128)(2,1)}, u32[]{:S(2)}, u32[]{:S(2)}) collective-permute-start(bf16[1,128,3,64]{3,1,2,0:T(8,128)(2,1)S(1)} %bitcast.156), channel_id=1, source_target_pairs={{16,0},{32,16},{48,32},{64,48},{80,64},{96,80},{112,96},{128,112},... | collective-permute-start | bytes 147464 | tf_op jit(solution)/shard_map/ppermute | solution.py:21
  31.8 451.0 %collective-permute-start.4 = (bf16[1,128,3,64]{3,1,2,0:T(8,128)(2,1)S(1)}, bf16[1,128,3,64]{3,1,2,0:T(8,128)(2,1)}, u32[]{:S(2)}, u32[]{:S(2)}) collective-permute-start(bf16[1,128,3,64]{3,1,2,0:T(8,128)(2,1)S(1)} %bitcast.157), channel_id=1, source_target_pairs={{0,16},{16,32},{32,48},{48,64},{64,80},{80,96},{96,112},{112,128},... | collective-permute-start | bytes 147464 | tf_op jit(solution)/shard_map/ppermute | solution.py:19
  57.7 426.3 %collective-permute-start.7 = (bf16[1,128,1024]{2,1,0:T(8,128)(2,1)S(1)}, bf16[1,128,1024]{2,1,0:T(8,128)(2,1)}, u32[]{:S(2)}, u32[]{:S(2)}) collective-permute-start(bf16[1,128,1024]{2,1,0:T(8,128)(2,1)S(1)} %bitcast.151), channel_id=1, source_target_pairs={{16,0},{32,16},{48,32},{64,48},{80,64},{96,80},{112,96},{128,112},... | collective-permute-start | bytes 786440 | tf_op jit(solution)/shard_map/ppermute | solution.py:21
  63.3 420.8 %collective-permute-start.6 = (bf16[1,128,1024]{2,1,0:T(8,128)(2,1)S(1)}, bf16[1,128,1024]{2,1,0:T(8,128)(2,1)}, u32[]{:S(2)}, u32[]{:S(2)}) collective-permute-start(bf16[1,128,1024]{2,1,0:T(8,128)(2,1)S(1)} %bitcast.152), channel_id=1, source_target_pairs={{0,16},{16,32},{32,48},{48,64},{64,80},{80,96},{96,112},{112,128},... | collective-permute-start | bytes 786440 | tf_op jit(solution)/shard_map/ppermute | solution.py:19
  92.6 385.6 %copy-start.1 = (bf16[1024,3,64]{2,1,0:T(4,128)(2,1)}, bf16[1024,3,64]{2,1,0:T(4,128)(2,1)S(1)}, u32[]{:S(2)}) copy-start(bf16[1024,3,64]{2,1,0:T(4,128)(2,1)S(1)} %all_gather.15) | copy-start | bytes 1179652
  93.8 458.3 %collective-permute-start.1 = (bf16[1,1024,3,64]{1,3,2,0:T(8,128)(2,1)}, bf16[1,1024,3,64]{1,3,2,0:T(8,128)(2,1)}, u32[]{:S(2)}, u32[]{:S(2)}) collective-permute-start(bf16[1,1024,3,64]{1,3,2,0:T(8,128)(2,1)} %copy.244), channel_id=1, source_target_pairs={{16,0},{32,16},{48,32},{64,48},{80,64},{96,80},{112,96},{128,112},... | collective-permute-start | bytes 1179656 | tf_op jit(solution)/shard_map/ppermute | solution.py:21
  101.9 378.3 %copy-start.5 = (bf16[1,64,512]{2,1,0:T(8,128)(2,1)S(1)}, bf16[1,64,512]{2,1,0:T(8,128)(2,1)}, u32[]{:S(2)}) copy-start(bf16[1,64,512]{2,1,0:T(8,128)(2,1)} %param.17) | copy-start | bytes 196612
  104.1 456.6 %all-to-all-start = ((bf16[256,2,512]{2,1,0:T(2,128)(2,1)}), bf16[256,2,512]{2,1,0:T(2,128)(2,1)}, u32[]{:S(2)}, u32[]{:S(2)}) async-start(bf16[256,2,512]{2,1,0:T(2,128)(2,1)} %reshape.319), calls=%async_computation | async-start | bytes 1048576 | tf_op jit(solution)/shard_map/all_to_all | solution.py:151
  480.9 72.9 %collective-permute-start = (bf16[1,1024,3,64]{1,3,2,0:T(8,128)(2,1)}, bf16[1,1024,3,64]{1,3,2,0:T(8,128)(2,1)}, u32[]{:S(2)}, u32[]{:S(2)}) collective-permute-start(bf16[1,1024,3,64]{1,3,2,0:T(8,128)(2,1)} %copy.244), channel_id=1, source_target_pairs={{0,16},{16,32},{32,48},{48,64},{64,80},{80,96},{96,112},{112,128},... | collective-permute-start | bytes 1179656 | tf_op jit(solution)/shard_map/ppermute | solution.py:19
  485.2 102.4 %collective-permute-start.3 = (bf16[1,1024,1024]{2,1,0:T(8,128)(2,1)}, bf16[1,1024,1024]{2,1,0:T(8,128)(2,1)}, u32[]{:S(2)}, u32[]{:S(2)}) collective-permute-start(bf16[1,1024,1024]{2,1,0:T(8,128)(2,1)} %bitcast.147), channel_id=1, source_target_pairs={{16,0},{32,16},{48,32},{64,48},{80,64},{96,80},{112,96},{128,112},... | collective-permute-start | bytes 6291464 | tf_op jit(solution)/shard_map/ppermute | solution.py:21
  492.2 95.4 %collective-permute-start.2 = (bf16[1,1024,1024]{2,1,0:T(8,128)(2,1)}, bf16[1,1024,1024]{2,1,0:T(8,128)(2,1)}, u32[]{:S(2)}, u32[]{:S(2)}) collective-permute-start(bf16[1,1024,1024]{2,1,0:T(8,128)(2,1)} %bitcast.148), channel_id=1, source_target_pairs={{0,16},{16,32},{32,48},{48,64},{64,80},{80,96},{96,112},{112,128},... | collective-permute-start | bytes 6291464 | tf_op jit(solution)/shard_map/ppermute | solution.py:19
  510.6 5.7 copy-start.11
  510.6 6.2 copy-start.6
  539.5 5.7 copy-start.11
  539.6 6.2 copy-start.6
  553.7 11.7 %copy-start.13 = (pred[96]{0:T(512)(128)(4,1)S(1)}, pred[96]{0:T(512)(128)(4,1)}, u32[]{:S(2)}) copy-start(pred[96]{0:T(512)(128)(4,1)} %compare_bitcast_fusion) | copy-start | bytes 292
  555.4 12.0 %copy-start.3 = (bf16[512,64]{1,0:T(8,128)(2,1)S(1)}, bf16[512,64]{1,0:T(8,128)(2,1)}, u32[]{:S(2)}) copy-start(bf16[512,64]{1,0:T(8,128)(2,1)} %copy.271) | copy-start | bytes 196612
  555.4 12.0 %copy-start.8 = (f32[2,4,64,16]{2,3,1,0:T(8,128)S(1)}, f32[2,4,64,16]{2,3,1,0:T(8,128)}, u32[]{:S(2)}) copy-start(f32[2,4,64,16]{2,3,1,0:T(8,128)} %get-tuple-element.101) | copy-start | bytes 98308
  560.7 6.7 copy-start.2
  (3 other events, 2.5 us)
Sparse Core Ops, SparseCore 0:
  10.7 40.2 all-gather.1
